TPU v7x, 32 devices: a whole 2x2x4 slice. The times are simulated.
32 devices in a mesh: group: 2 (over x), inst: 8 (over z, y), tp: 2 (over core).
Axes of the slice: x: 2, y: 2, z: 4, core: 2. Of those that a mesh axis runs over, the one named last changes fastest.
Arguments:
- kv_pool: bfloat16 [2560, 16, 2, 1024], P(('group', 'inst'), None, None, 'tp'), parts along dimension 0, may hold values from -5 to 5
- page_table: int32 [160, 16], P(('group', 'inst')), parts along dimension 0, may hold values from 0 to 159, as said below
- lengths: int32 [160], P(('group', 'inst')), parts along dimension 0, may hold values from 0 to 252, as said below
- move_source: int32 [16, 4, 2], P(('group', 'inst')), parts along dimension 0, may hold values from -1 to 9, as said below
- move_slot: int32 [16, 4, 2], P(('group', 'inst')), parts along dimension 0, may hold values from -1 to 9, as said below
- queries: bfloat16 [4, 160, 8192], P(None, ('group', 'inst'), 'tp'), parts along dimension 1, may hold values from -5 to 5
- new_kv: bfloat16 [4, 160, 2, 1024], P(None, ('group', 'inst'), None, 'tp'), parts along dimension 1, may hold values from -5 to 5
Outputs:
- attended: bfloat16 [4, 160, 8192], P(None, ('group', 'inst'), 'tp'), parts along dimension 1
- cache_after: bfloat16 [2560, 16, 2, 1024], P(('group', 'inst'), None, None, 'tp'), parts along dimension 0
There are 2 independent parts, one for each index of `group`. A program takes and returns all parts, laid end to end along the dimension named above; each array names one. Nothing has to cross between parts.
Inputs may be any that keep to these rules, and one draw needn't show every extreme that they name: `page_table`: the 16 entries of the 10 rows of one instance name each of that instance's 160 pages once. `lengths`: every length plus 4 fits the row's 16 pages. At step s instance i sends at most one row to each side e, the live row in slot move_source[i, s, e] (-1: none), to instance i + 1 modulo 8 for side 0 and i - 1 modulo 8 for side 1. A slot sends at most once, a slot that a row leaves stays empty, and a row that arrives is never sent on. `move_slot`: the receiving slot is empty (length 0) until the row arrives and receives no other row (-1 where nothing is sent).
All inputs are finite; a program needn't handle non-finite values.
Results may differ from a plain program's by a relative error of at most 0.0039.
Values may be sent and summed in bfloat16 or wider, within the bound.
A program may use at most 128 MiB of HBM per device.

v0:
```python
import functools

import jax
import jax.numpy as jnp
from jax import lax
from jax.experimental import pallas as pl
from jax.experimental.pallas import tpu as pltpu
from jax.sharding import PartitionSpec as P

HD = 128
SMEM = pl.BlockSpec(memory_space=pltpu.SMEM)
VMEM = pl.BlockSpec(memory_space=pltpu.VMEM)
ANY = pl.BlockSpec(memory_space=pl.ANY)


def pack_kernel(step, table, lengths, source, pool, fresh, left, right, page_sem, token_sem):
    ctx_pages = table.shape[1]
    page_len = pool.shape[1]
    outs = (left, right)

    def one_page(p, carry):
        for side in range(2):
            slot = jnp.maximum(source[0, step, side], 0)
            pltpu.make_async_copy(
                pool.at[table[slot, p]],
                outs[side].at[pl.ds(p * page_len, page_len)],
                page_sem.at[side],
            ).start()
        return carry

    lax.fori_loop(0, ctx_pages, one_page, 0)
    for side in range(2):
        pltpu.make_async_copy(outs[side], outs[side], page_sem.at[side]).wait()
    copies = []
    for side in range(2):
        slot = jnp.maximum(source[0, step, side], 0)
        for early in range(step):
            copies.append(
                pltpu.make_async_copy(
                    fresh.at[early, slot],
                    outs[side].at[lengths[slot] + early],
                    token_sem.at[side, early],
                )
            )
    for copy in copies:
        copy.start()
    for copy in copies:
        copy.wait()


def pack(step, table, lengths, source, pool, fresh):
    tokens = table.shape[1] * pool.shape[1]
    row = jax.ShapeDtypeStruct((tokens,) + pool.shape[2:], pool.dtype)
    nbytes = 4 * tokens * pool.shape[2] * pool.shape[3] * 2
    return pl.pallas_call(
        functools.partial(pack_kernel, step),
        out_shape=(row, row),
        in_specs=[SMEM, SMEM, SMEM, ANY, ANY],
        out_specs=(ANY, ANY),
        scratch_shapes=[pltpu.SemaphoreType.DMA((2,)), pltpu.SemaphoreType.DMA((2, fresh.shape[0]))],
        cost_estimate=pl.CostEstimate(flops=0, bytes_accessed=nbytes, transcendentals=0),
    )(table, lengths, source, pool, fresh)


def attend(rows, query, out, slot, base, first, low, high):
    kv_heads, columns, _ = rows.shape
    total_rows = query.shape[2]
    steps = out.shape[0]
    group = total_rows // steps
    skip = first * group
    shape = (total_rows - skip, columns)
    row_step = lax.broadcasted_iota(jnp.int32, shape, 0) // group + first
    column = lax.broadcasted_iota(jnp.int32, shape, 1)
    seen = (column % 2 == 0) & (column // 2 <= base + row_step)
    step_of = lax.broadcasted_iota(jnp.int32, (shape[0], HD), 0) // group + first
    live = (step_of >= low) & (step_of < high)
    chosen = lax.broadcasted_iota(jnp.int32, (out.shape[1], HD), 0) == slot
    for head in range(kv_heads):
        matrix = rows[head]
        q = query[slot, head, skip:]
        scores = lax.dot_general(
            q, matrix, (((1,), (1,)), ((), ())), preferred_element_type=jnp.float32
        ) * HD ** (-0.5)
        scores = jnp.where(seen, scores, -jnp.inf)
        terms = jnp.exp(scores - jnp.max(scores, axis=1, keepdims=True))
        total = jnp.sum(terms, axis=1, keepdims=True)
        weights = pltpu.roll(terms, 1, 1).astype(jnp.bfloat16)
        result = jnp.dot(weights, matrix, preferred_element_type=jnp.float32) / total
        result = jnp.where(live, result, 0.0)
        for s in range(first, steps):
            for g in range(group):
                r = (s - first) * group + g
                lane = (head * group + g) * HD
                old = out[s, :, lane : lane + HD]
                out[s, :, lane : lane + HD] = jnp.where(chosen, result[r : r + 1], old)


def local_kernel(table, lengths, source, pool, fresh, query, cache, attended, rows, out, copy_sem, row_sem, token_sem):
    slots, ctx_pages = table.shape
    pages, page_len = pool.shape[:2]
    kv_heads = rows.shape[1]
    steps = fresh.shape[0]
    part = pages // slots

    def load_slot(c, carry):
        pltpu.make_async_copy(
            pool.at[pl.ds(c * part, part)], cache.at[pl.ds(c * part, part)], copy_sem
        ).start()

        def load_page(p, carry):
            for head in range(kv_heads):
                pltpu.make_async_copy(
                    pool.at[table[c, p], :, :, pl.ds(head * HD, HD)],
                    rows.at[c, head, pl.ds(p * page_len, page_len)],
                    row_sem.at[c],
                ).start()
            return carry

        return lax.fori_loop(0, ctx_pages, load_page, carry)

    lax.fori_loop(0, slots, load_slot, 0)

    def leave_step(c):
        leave = jnp.int32(steps)
        for s in range(steps):
            for side in range(2):
                leave = jnp.where(source[0, s, side] == c, s, leave)
        return jnp.where(lengths[c] > 0, leave, 0)

    def work(c, carry):
        pltpu.make_async_copy(rows.at[c], rows.at[c], row_sem.at[c]).wait()
        base = lengths[c]
        for s in range(steps):
            for head in range(kv_heads):
                rows[c, head, base + s] = fresh[s, c, :, head * HD : (head + 1) * HD]
        attend(
            rows.at[c].reshape(kv_heads, ctx_pages * page_len * 2, HD), query, out, c, base, 0, 0, leave_step(c)
        )
        return carry

    lax.fori_loop(0, slots, work, 0)
    pltpu.make_async_copy(cache, cache, copy_sem).wait()

    def token(c, s):
        pos = lengths[c] + s
        return pltpu.make_async_copy(
            fresh.at[s, c], cache.at[table[c, pos // page_len], pos % page_len], token_sem.at[c, s]
        )

    def start(c, carry):
        high = leave_step(c)
        for s in range(steps):

            @pl.when(s < high)
            def _():
                token(c, s).start()

        return carry

    def finish(c, carry):
        high = leave_step(c)
        for s in range(steps):

            @pl.when(s < high)
            def _():
                token(c, s).wait()

        return carry

    lax.fori_loop(0, slots, start, 0)
    attended[...] = out[...].astype(attended.dtype)
    lax.fori_loop(0, slots, finish, 0)


def local(table, lengths, source, pool, fresh, query):
    slots, ctx_pages = table.shape
    tokens = ctx_pages * pool.shape[1]
    kv_heads = query.shape[1]
    steps = fresh.shape[0]
    width = kv_heads * query.shape[2] // steps * HD
    return pl.pallas_call(
        local_kernel,
        out_shape=(
            jax.ShapeDtypeStruct(pool.shape, pool.dtype),
            jax.ShapeDtypeStruct((steps, slots, width), jnp.bfloat16),
        ),
        in_specs=[SMEM, SMEM, SMEM, ANY, VMEM, VMEM],
        out_specs=(ANY, VMEM),
        scratch_shapes=[
            pltpu.VMEM((slots, kv_heads, tokens, 2, HD), pool.dtype),
            pltpu.VMEM((steps, slots, width), jnp.float32),
            pltpu.SemaphoreType.DMA,
            pltpu.SemaphoreType.DMA((slots,)),
            pltpu.SemaphoreType.DMA((slots, steps)),
        ],
        compiler_params=pltpu.CompilerParams(vmem_limit_bytes=32 * 1024 * 1024),
        cost_estimate=pl.CostEstimate(flops=10**9, bytes_accessed=60 * 10**6, transcendentals=10**5),
    )(table, lengths, source, pool, fresh, query)


def arrive_kernel(step, table, meta_left, meta_right, left, right, fresh, query, cache_in, before, cache, attended, rows, out, page_sem, row_sem, token_sem):
    ctx_pages = table.shape[1]
    page_len = cache.shape[1]
    kv_heads = rows.shape[1]
    steps = fresh.shape[0]
    received = (left, right)
    metas = (meta_left, meta_right)

    def token(side, s, slot, base):
        pos = base + s
        return pltpu.make_async_copy(
            fresh.at[s, slot], cache.at[table[slot, pos // page_len], pos % page_len], token_sem.at[side, s]
        )

    for side in range(2):
        slot = metas[side][step, 0] - 1

        @pl.when(slot >= 0)
        def _():
            for head in range(kv_heads):
                pltpu.make_async_copy(
                    received[side].at[:, :, pl.ds(head * HD, HD)], rows.at[side, head], row_sem.at[side]
                ).start()

            def store_page(p, carry):
                pltpu.make_async_copy(
                    received[side].at[pl.ds(p * page_len, page_len)], cache.at[table[slot, p]], page_sem.at[side]
                ).start()
                return carry

            lax.fori_loop(0, ctx_pages, store_page, 0)

    out[...] = before[...].astype(jnp.float32)
    for side in range(2):
        slot = metas[side][step, 0] - 1
        base = metas[side][step, 1]

        @pl.when(slot >= 0)
        def _():
            pltpu.make_async_copy(rows.at[side], rows.at[side], row_sem.at[side]).wait()
            for s in range(step, steps):
                for head in range(kv_heads):
                    rows[side, head, base + s] = fresh[s, slot, :, head * HD : (head + 1) * HD]
            pltpu.make_async_copy(received[side], received[side], page_sem.at[side]).wait()
            for s in range(step, steps):
                token(side, s, slot, base).start()
            attend(
                rows.at[side].reshape(kv_heads, ctx_pages * page_len * 2, HD),
                query, out, slot, base, step, step, steps,
            )

    attended[...] = out[...].astype(attended.dtype)
    for side in range(2):
        slot = metas[side][step, 0] - 1
        base = metas[side][step, 1]

        @pl.when(slot >= 0)
        def _():
            for s in range(step, steps):
                token(side, s, slot, base).wait()


def arrive(step, table, meta_left, meta_right, left, right, fresh, query, cache, attended):
    tokens = left.shape[0]
    kv_heads = query.shape[1]
    steps = fresh.shape[0]
    return pl.pallas_call(
        functools.partial(arrive_kernel, step),
        out_shape=(
            jax.ShapeDtypeStruct(cache.shape, cache.dtype),
            jax.ShapeDtypeStruct(attended.shape, attended.dtype),
        ),
        in_specs=[SMEM, SMEM, SMEM, ANY, ANY, VMEM, VMEM, ANY, VMEM],
        out_specs=(ANY, VMEM),
        input_output_aliases={7: 0},
        scratch_shapes=[
            pltpu.VMEM((2, kv_heads, tokens, 2, HD), cache.dtype),
            pltpu.VMEM(attended.shape, jnp.float32),
            pltpu.SemaphoreType.DMA((2,)),
            pltpu.SemaphoreType.DMA((2,)),
            pltpu.SemaphoreType.DMA((2, steps)),
        ],
        compiler_params=pltpu.CompilerParams(vmem_limit_bytes=32 * 1024 * 1024),
        cost_estimate=pl.CostEstimate(flops=10**8, bytes_accessed=10 * 10**6, transcendentals=10**5),
    )(table, meta_left, meta_right, left, right, fresh, query, cache, attended)


def body(kv_pool, page_table, lengths, move_source, move_slot, queries, new_kv):
    slots = page_table.shape[0]
    steps = queries.shape[0]
    kv_heads = kv_pool.shape[3] // HD
    group = queries.shape[2] // HD // kv_heads
    count = lax.axis_size("inst")

    def shift(value, by):
        return lax.ppermute(value, "inst", [(i, (i + by) % count) for i in range(count)])

    arrived = []
    for step in range(steps):
        up, down = pack(step, page_table, lengths, move_source, kv_pool, new_kv)
        if step == 0:
            up, down, queries, move_slot = lax.optimization_barrier((up, down, queries, move_slot))
        arrived.append((shift(up, 1), shift(down, -1)))
    length = lengths[jnp.maximum(move_source[0], 0)]
    meta = jnp.stack([jnp.where(move_source[0] >= 0, move_slot[0] + 1, 0), length], axis=2)
    meta_left = shift(meta[:, 0], 1)
    meta_right = shift(meta[:, 1], -1)
    query = queries.reshape(steps, slots, kv_heads, group, HD).transpose(1, 2, 0, 3, 4)
    query = query.reshape(slots, kv_heads, steps * group, HD)
    cache, attended = local(page_table, lengths, move_source, kv_pool, new_kv, query)
    for step in range(steps):
        cache, attended = arrive(
            step, page_table, meta_left, meta_right, *arrived[step], new_kv, query, cache, attended
        )
    return attended, cache


def solution(mesh):
    in_specs = (
        P(("group", "inst"), None, None, "tp"),
        P(("group", "inst"), None),
        P(("group", "inst")),
        P(("group", "inst"), None, None),
        P(("group", "inst"), None, None),
        P(None, ("group", "inst"), "tp"),
        P(None, ("group", "inst"), None, "tp"),
    )
    out_specs = (P(None, ("group", "inst"), "tp"), P(("group", "inst"), None, None, "tp"))
    return jax.shard_map(body, mesh=mesh, in_specs=in_specs, out_specs=out_specs, check_vma=False)
```

profile of v0, /device:TPU:0, one launch (start us, length us, event | category | flops | bytes accessed | tf_op | source)
XLA Modules:
  0.0 250.9 jit_solution(11785416760700478534)
XLA Ops:
  0.6 1.3 copy.24.source
  2.0 0.0 copy-start.6
  2.0 0.0 copy-start.7
  2.0 0.0 copy-start
  2.0 33.9 %shard_map.86 = (bf16[256,2,512]{2,1,0:T(2,128)(2,1)}, bf16[256,2,512]{2,1,0:T(2,128)(2,1)}) custom-call(s32[10,16]{1,0:T(8,128)} %table.17, s32[10]{0:T(128)} %lengths.9, s32[1,4,2]{2,1,0:T(4,128)} %copy.24.source, bf16[160,16,2,512]{3,2,1,0:T(2,128)(2,1)} %pool.9, bf16[4,10,2,512]{3,2,1,0:T(2,128)(2,1)} %fresh.17), custom_call_target="tpu_custom_call" | custom-call | bytes 2097152 | tf_op jit(solution)/shard_map/pallas_call | solution.py:55
  35.9 3.0 %collective-permute-start.8 = (bf16[256,2,512]{2,1,0:T(2,128)(2,1)}, bf16[256,2,512]{2,1,0:T(2,128)(2,1)S(1)}, u32[]{:S(2)}, u32[]{:S(2)}) collective-permute-start(bf16[256,2,512]{2,1,0:T(2,128)(2,1)} %get-tuple-element.34), channel_id=1, source_target_pairs={{0,2},{2,4},{4,6},{6,8},{8,10},{10,12},{12,14},{14,0},{1,3},{3,5},... | collective-permute-start | bytes 1572872 | tf_op jit(solution)/shard_map/ppermute | solution.py:296
  38.9 3.1 %collective-permute-start.9 = (bf16[256,2,512]{2,1,0:T(2,128)(2,1)}, bf16[256,2,512]{2,1,0:T(2,128)(2,1)S(1)}, u32[]{:S(2)}, u32[]{:S(2)}) collective-permute-start(bf16[256,2,512]{2,1,0:T(2,128)(2,1)} %get-tuple-element.35), channel_id=1, source_target_pairs={{0,14},{2,0},{4,2},{6,4},{8,6},{10,8},{12,10},{14,12},{1,15},{3,1}... | collective-permute-start | bytes 1572872 | tf_op jit(solution)/shard_map/ppermute | solution.py:296
  42.0 35.0 %shard_map.89 = (bf16[256,2,512]{2,1,0:T(2,128)(2,1)}, bf16[256,2,512]{2,1,0:T(2,128)(2,1)}) custom-call(s32[10,16]{1,0:T(8,128)} %table.17, s32[10]{0:T(128)} %lengths.9, s32[1,4,2]{2,1,0:T(4,128)} %copy.24.source, bf16[160,16,2,512]{3,2,1,0:T(2,128)(2,1)} %pool.9, bf16[4,10,2,512]{3,2,1,0:T(2,128)(2,1)} %fresh.17), custom_call_target="tpu_custom_call" | custom-call | bytes 2097152 | tf_op jit(solution)/shard_map/pallas_call | solution.py:55
  77.1 0.1 collective-permute-start.6
  77.1 4.7 %collective-permute-start.7 = (bf16[256,2,512]{2,1,0:T(2,128)(2,1)}, bf16[256,2,512]{2,1,0:T(2,128)(2,1)S(1)}, u32[]{:S(2)}, u32[]{:S(2)}) collective-permute-start(bf16[256,2,512]{2,1,0:T(2,128)(2,1)} %get-tuple-element.33), channel_id=1, source_target_pairs={{0,14},{2,0},{4,2},{6,4},{8,6},{10,8},{12,10},{14,12},{1,15},{3,1}... | collective-permute-start | bytes 1572872 | tf_op jit(solution)/shard_map/ppermute | solution.py:296
  81.8 0.0 copy-done.6
  81.8 0.0 copy-done.7
  81.9 0.1 copy.25
  81.9 0.1 reshape.55
  82.0 0.0 copy-done
  82.0 0.6 gather_fusion
  82.7 0.1 stack.7
  82.8 0.1 copy.26
  82.9 0.1 copy.27
  83.0 0.0 copy-start.1
  83.0 0.0 copy-start.3
  83.0 0.0 copy-start.4
  83.0 0.0 copy-start.5
  83.0 0.1 collective-permute-start
  83.1 35.1 %shard_map.88 = (bf16[256,2,512]{2,1,0:T(2,128)(2,1)}, bf16[256,2,512]{2,1,0:T(2,128)(2,1)}) custom-call(s32[10,16]{1,0:T(8,128)} %table.17, s32[10]{0:T(128)} %lengths.9, s32[1,4,2]{2,1,0:T(4,128)} %copy.24.source, bf16[160,16,2,512]{3,2,1,0:T(2,128)(2,1)} %pool.9, bf16[4,10,2,512]{3,2,1,0:T(2,128)(2,1)} %fresh.17), custom_call_target="tpu_custom_call" | custom-call | bytes 2097152 | tf_op jit(solution)/shard_map/pallas_call | solution.py:55
  118.2 0.1 copy.28
  118.3 0.0 collective-permute-done.meta_left
  118.3 4.7 %collective-permute-start.1 = (s32[4,2]{1,0:T(4,128)S(1)}, s32[4,2]{1,0:T(4,128)S(1)}, u32[]{:S(2)}, u32[]{:S(2)}) collective-permute-start(s32[4,2]{1,0:T(4,128)S(1)} %copy.28), channel_id=1, source_target_pairs={{0,14},{2,0},{4,2},{6,4},{8,6},{10,8},{12,10},{14,12},{1,15},{3,1}... | collective-permute-start | bytes 104 | tf_op jit(solution)/shard_map/ppermute | solution.py:296
  123.0 1.3 collective-permute-done.1.meta_right
  124.3 0.0 collective-permute-start.4
  124.3 0.0 collective-permute-done.8.left
  124.3 5.0 %collective-permute-start.5 = (bf16[256,2,512]{2,1,0:T(2,128)(2,1)}, bf16[256,2,512]{2,1,0:T(2,128)(2,1)}, u32[]{:S(2)}, u32[]{:S(2)}) collective-permute-start(bf16[256,2,512]{2,1,0:T(2,128)(2,1)} %get-tuple-element.31), channel_id=1, source_target_pairs={{0,14},{2,0},{4,2},{6,4},{8,6},{10,8},{12,10},{14,12},{1,15},{3,1}... | collective-permute-start | bytes 1572872 | tf_op jit(solution)/shard_map/ppermute | solution.py:296
  129.3 35.3 %shard_map.87 = (bf16[256,2,512]{2,1,0:T(2,128)(2,1)}, bf16[256,2,512]{2,1,0:T(2,128)(2,1)}) custom-call(s32[10,16]{1,0:T(8,128)} %table.17, s32[10]{0:T(128)} %lengths.9, s32[1,4,2]{2,1,0:T(4,128)} %copy.24.source, bf16[160,16,2,512]{3,2,1,0:T(2,128)(2,1)} %pool.9, bf16[4,10,2,512]{3,2,1,0:T(2,128)(2,1)} %fresh.17), custom_call_target="tpu_custom_call" | custom-call | bytes 2097152 | tf_op jit(solution)/shard_map/pallas_call | solution.py:55
  164.6 0.0 collective-permute-done.9.right
  164.6 0.1 collective-permute-start.2
  164.7 0.0 collective-permute-done.6.left
  164.7 4.7 %collective-permute-start.3 = (bf16[256,2,512]{2,1,0:T(2,128)(2,1)}, bf16[256,2,512]{2,1,0:T(2,128)(2,1)}, u32[]{:S(2)}, u32[]{:S(2)}) collective-permute-start(bf16[256,2,512]{2,1,0:T(2,128)(2,1)} %get-tuple-element.28), channel_id=1, source_target_pairs={{0,14},{2,0},{4,2},{6,4},{8,6},{10,8},{12,10},{14,12},{1,15},{3,1}... | collective-permute-start | bytes 1572872 | tf_op jit(solution)/shard_map/ppermute | solution.py:296
  169.4 2.0 reshape.51
  171.4 1.0 copy.36
  172.4 0.0 copy-done.1
  172.5 0.0 copy-done.3
  172.5 0.0 copy-done.4
  172.5 0.0 copy-done.5
  172.5 0.0 copy-start.2
  172.5 2.5 copy-done.2
  175.0 24.4 %shard_map.90 = (bf16[160,16,2,512]{3,2,1,0:T(2,128)(2,1)}, bf16[4,10,4096]{2,1,0:T(8,128)(2,1)S(1)}) custom-call(s32[10,16]{1,0:T(8,128)S(1)} %copy-done.4, s32[10]{0:T(128)S(1)} %copy-done.1, s32[1,4,2]{2,1,0:T(4,128)S(1)} %copy-done.5, bf16[160,16,2,512]{3,2,1,0:T(2,128)(2,1)S(1)} %copy-done.2, bf16[4,10,2,512]{3,2,1,0:T(2,128)(2,1)S(1)} %copy-done.3, ...), custom_call_target="tpu_custom_call" | custom-call | flops 1000000000 | bytes 60000000 | tf_op jit(solution)/shard_map/pallas_call | solution.py:181
  199.4 5.3 %shard_map.91 = (bf16[160,16,2,512]{3,2,1,0:T(2,128)(2,1)}, bf16[4,10,4096]{2,1,0:T(8,128)(2,1)S(1)}) custom-call(s32[10,16]{1,0:T(8,128)S(1)} %copy-done.4, s32[4,2]{1,0:T(4,128)S(1)} %collective-permute-done.meta_left, s32[4,2]{1,0:T(4,128)S(1)} %collective-permute-done.1.meta_right, ...), custom_call_target="tpu_custom_call", output_to_operand_aliasing={{0}: (7, {})} | custom-call | flops 100000000 | bytes 10000000 | tf_op jit(solution)/shard_map/pallas_call | solution.py:267
  204.7 0.0 collective-permute-done.7.right
  204.7 5.3 %shard_map.92 = (bf16[160,16,2,512]{3,2,1,0:T(2,128)(2,1)}, bf16[4,10,4096]{2,1,0:T(8,128)(2,1)S(1)}) custom-call(s32[10,16]{1,0:T(8,128)S(1)} %copy-done.4, s32[4,2]{1,0:T(4,128)S(1)} %collective-permute-done.meta_left, s32[4,2]{1,0:T(4,128)S(1)} %collective-permute-done.1.meta_right, ...), custom_call_target="tpu_custom_call", output_to_operand_aliasing={{0}: (7, {})} | custom-call | flops 100000000 | bytes 10000000 | tf_op jit(solution)/shard_map/pallas_call | solution.py:267
  209.9 0.0 collective-permute-done.4.left
  209.9 0.0 collective-permute-done.5.right
  210.0 20.1 %shard_map.93 = (bf16[160,16,2,512]{3,2,1,0:T(2,128)(2,1)}, bf16[4,10,4096]{2,1,0:T(8,128)(2,1)S(1)}) custom-call(s32[10,16]{1,0:T(8,128)S(1)} %copy-done.4, s32[4,2]{1,0:T(4,128)S(1)} %collective-permute-done.meta_left, s32[4,2]{1,0:T(4,128)S(1)} %collective-permute-done.1.meta_right, ...), custom_call_target="tpu_custom_call", output_to_operand_aliasing={{0}: (7, {})} | custom-call | flops 100000000 | bytes 10000000 | tf_op jit(solution)/shard_map/pallas_call | solution.py:267
  230.1 0.0 collective-permute-done.2.left
  230.1 0.0 collective-permute-done.3.right
  230.1 19.8 %shard_map.94 = (bf16[160,16,2,512]{3,2,1,0:T(2,128)(2,1)}, bf16[4,10,4096]{2,1,0:T(8,128)(2,1)S(1)}) custom-call(s32[10,16]{1,0:T(8,128)S(1)} %copy-done.4, s32[4,2]{1,0:T(4,128)S(1)} %collective-permute-done.meta_left, s32[4,2]{1,0:T(4,128)S(1)} %collective-permute-done.1.meta_right, ...), custom_call_target="tpu_custom_call", output_to_operand_aliasing={{0}: (7, {})} | custom-call | flops 100000000 | bytes 10000000 | tf_op jit(solution)/shard_map/pallas_call | solution.py:267
  249.9 1.0 copy.34
  (3 shorter events, 0.0 us)
Async XLA Ops:
  2.0 79.9 %copy-start.6 = (s32[1,4,2]{1,2,0:T(2,128)S(1)}, s32[1,4,2]{1,2,0:T(2,128)}, u32[]{:S(2)}) copy-start(s32[1,4,2]{1,2,0:T(2,128)} %param.10) | copy-start | bytes 100
  2.0 79.9 %copy-start.7 = (s32[1,4,2]{1,2,0:T(2,128)S(1)}, s32[1,4,2]{1,2,0:T(2,128)}, u32[]{:S(2)}) copy-start(s32[1,4,2]{1,2,0:T(2,128)} %param.11) | copy-start | bytes 100
  2.0 80.1 %copy-start = (s32[10]{0:T(128)S(1)}, s32[10]{0:T(128)}, u32[]{:S(2)}) copy-start(s32[10]{0:T(128)} %lengths.9) | copy-start | bytes 124
  35.9 88.4 %collective-permute-start.8 = (bf16[256,2,512]{2,1,0:T(2,128)(2,1)}, bf16[256,2,512]{2,1,0:T(2,128)(2,1)S(1)}, u32[]{:S(2)}, u32[]{:S(2)}) collective-permute-start(bf16[256,2,512]{2,1,0:T(2,128)(2,1)} %get-tuple-element.34), channel_id=1, source_target_pairs={{0,2},{2,4},{4,6},{6,8},{8,10},{10,12},{12,14},{14,0},{1,3},{3,5},... | collective-permute-start | bytes 1572872 | tf_op jit(solution)/shard_map/ppermute | solution.py:296
  38.9 125.6 %collective-permute-start.9 = (bf16[256,2,512]{2,1,0:T(2,128)(2,1)}, bf16[256,2,512]{2,1,0:T(2,128)(2,1)S(1)}, u32[]{:S(2)}, u32[]{:S(2)}) collective-permute-start(bf16[256,2,512]{2,1,0:T(2,128)(2,1)} %get-tuple-element.35), channel_id=1, source_target_pairs={{0,14},{2,0},{4,2},{6,4},{8,6},{10,8},{12,10},{14,12},{1,15},{3,1}... | collective-permute-start | bytes 1572872 | tf_op jit(solution)/shard_map/ppermute | solution.py:296
  77.1 87.6 %collective-permute-start.6 = (bf16[256,2,512]{2,1,0:T(2,128)(2,1)}, bf16[256,2,512]{2,1,0:T(2,128)(2,1)S(1)}, u32[]{:S(2)}, u32[]{:S(2)}) collective-permute-start(bf16[256,2,512]{2,1,0:T(2,128)(2,1)} %get-tuple-element.32), channel_id=1, source_target_pairs={{0,2},{2,4},{4,6},{6,8},{8,10},{10,12},{12,14},{14,0},{1,3},{3,5},... | collective-permute-start | bytes 1572872 | tf_op jit(solution)/shard_map/ppermute | solution.py:296
  77.1 127.5 %collective-permute-start.7 = (bf16[256,2,512]{2,1,0:T(2,128)(2,1)}, bf16[256,2,512]{2,1,0:T(2,128)(2,1)S(1)}, u32[]{:S(2)}, u32[]{:S(2)}) collective-permute-start(bf16[256,2,512]{2,1,0:T(2,128)(2,1)} %get-tuple-element.33), channel_id=1, source_target_pairs={{0,14},{2,0},{4,2},{6,4},{8,6},{10,8},{12,10},{14,12},{1,15},{3,1}... | collective-permute-start | bytes 1572872 | tf_op jit(solution)/shard_map/ppermute | solution.py:296
  83.0 89.5 %copy-start.1 = (s32[10]{0:T(128)S(1)}, s32[10]{0:T(128)}, u32[]{:S(2)}) copy-start(s32[10]{0:T(128)} %lengths.9) | copy-start | bytes 124
  83.0 89.5 %copy-start.3 = (bf16[4,10,2,512]{3,2,1,0:T(2,128)(2,1)S(1)}, bf16[4,10,2,512]{3,2,1,0:T(2,128)(2,1)}, u32[]{:S(2)}) copy-start(bf16[4,10,2,512]{3,2,1,0:T(2,128)(2,1)} %fresh.17) | copy-start | bytes 245764
  83.0 89.5 %copy-start.4 = (s32[10,16]{1,0:T(8,128)S(1)}, s32[10,16]{1,0:T(8,128)}, u32[]{:S(2)}) copy-start(s32[10,16]{1,0:T(8,128)} %table.17) | copy-start | bytes 1924
  83.0 89.5 %copy-start.5 = (s32[1,4,2]{2,1,0:T(4,128)S(1)}, s32[1,4,2]{2,1,0:T(4,128)}, u32[]{:S(2)}) copy-start(s32[1,4,2]{2,1,0:T(4,128)} %copy.24.source) | copy-start | bytes 100
  83.0 35.3 %collective-permute-start = (s32[4,2]{1,0:T(4,128)S(1)}, s32[4,2]{1,0:T(4,128)S(1)}, u32[]{:S(2)}, u32[]{:S(2)}) collective-permute-start(s32[4,2]{1,0:T(4,128)S(1)} %copy.27), channel_id=1, source_target_pairs={{0,2},{2,4},{4,6},{6,8},{8,10},{10,12},{12,14},{14,0},{1,3},{3,5},... | collective-permute-start | bytes 104 | tf_op jit(solution)/shard_map/ppermute | solution.py:296
  118.3 6.0 %collective-permute-start.1 = (s32[4,2]{1,0:T(4,128)S(1)}, s32[4,2]{1,0:T(4,128)S(1)}, u32[]{:S(2)}, u32[]{:S(2)}) collective-permute-start(s32[4,2]{1,0:T(4,128)S(1)} %copy.28), channel_id=1, source_target_pairs={{0,14},{2,0},{4,2},{6,4},{8,6},{10,8},{12,10},{14,12},{1,15},{3,1}... | collective-permute-start | bytes 104 | tf_op jit(solution)/shard_map/ppermute | solution.py:296
  124.3 85.6 %collective-permute-start.4 = (bf16[256,2,512]{2,1,0:T(2,128)(2,1)}, bf16[256,2,512]{2,1,0:T(2,128)(2,1)S(1)}, u32[]{:S(2)}, u32[]{:S(2)}) collective-permute-start(bf16[256,2,512]{2,1,0:T(2,128)(2,1)} %get-tuple-element.30), channel_id=1, source_target_pairs={{0,2},{2,4},{4,6},{6,8},{8,10},{10,12},{12,14},{14,0},{1,3},{3,5},... | collective-permute-start | bytes 1572872 | tf_op jit(solution)/shard_map/ppermute | solution.py:296
  124.3 85.6 %collective-permute-start.5 = (bf16[256,2,512]{2,1,0:T(2,128)(2,1)}, bf16[256,2,512]{2,1,0:T(2,128)(2,1)}, u32[]{:S(2)}, u32[]{:S(2)}) collective-permute-start(bf16[256,2,512]{2,1,0:T(2,128)(2,1)} %get-tuple-element.31), channel_id=1, source_target_pairs={{0,14},{2,0},{4,2},{6,4},{8,6},{10,8},{12,10},{14,12},{1,15},{3,1}... | collective-permute-start | bytes 1572872 | tf_op jit(solution)/shard_map/ppermute | solution.py:296
  164.6 65.5 %collective-permute-start.2 = (bf16[256,2,512]{2,1,0:T(2,128)(2,1)}, bf16[256,2,512]{2,1,0:T(2,128)(2,1)S(1)}, u32[]{:S(2)}, u32[]{:S(2)}) collective-permute-start(bf16[256,2,512]{2,1,0:T(2,128)(2,1)} %get-tuple-element.27), channel_id=1, source_target_pairs={{0,2},{2,4},{4,6},{6,8},{8,10},{10,12},{12,14},{14,0},{1,3},{3,5},... | collective-permute-start | bytes 1572872 | tf_op jit(solution)/shard_map/ppermute | solution.py:296
  164.7 65.4 %collective-permute-start.3 = (bf16[256,2,512]{2,1,0:T(2,128)(2,1)}, bf16[256,2,512]{2,1,0:T(2,128)(2,1)}, u32[]{:S(2)}, u32[]{:S(2)}) collective-permute-start(bf16[256,2,512]{2,1,0:T(2,128)(2,1)} %get-tuple-element.28), channel_id=1, source_target_pairs={{0,14},{2,0},{4,2},{6,4},{8,6},{10,8},{12,10},{14,12},{1,15},{3,1}... | collective-permute-start | bytes 1572872 | tf_op jit(solution)/shard_map/ppermute | solution.py:296
  172.5 2.5 copy-start.2
where the time goes:
time: 251 us
  Pallas kernels  214 us (85%)
  starting transfers between devices  25.4 us (10%)
  local copies, waits for them, and re-layouts  9.1 us (4%)
    pallas_call x4, Pallas kernels, pack(): pl.pallas_call(functools.partial(pack_kernel, step), out_shape=(row, row)...  139 us
    pallas_call x4, Pallas kernels, arrive(): pl.pallas_call(functools.partial(arrive_kernel, step), out_shape=(jax.Sha...  50.4 us
    ppermute x10, starting transfers between devices, shift(): lax.ppermute(value, 'inst', [(i, (i + by) % count) for i in range(count)])  25.4 us
    pallas_call x1, Pallas kernels, local(): pl.pallas_call(local_kernel, out_shape=(jax.ShapeDtypeStruct(pool.shape,...  24.4 us
  transfers between devices with their start and end apart: 10, of which 1 were waited for; matrix products, arithmetic and copies ran while one was open for 2% of the time, Pallas kernels for 64%

commit v1 on v0

v1 whole, which is shorter than its diff:
```python
import functools

import jax
import jax.numpy as jnp
from jax import lax
from jax.experimental import pallas as pl
from jax.experimental.pallas import tpu as pltpu
from jax.sharding import PartitionSpec as P

HD = 128
SMEM = pl.BlockSpec(memory_space=pltpu.SMEM)
VMEM = pl.BlockSpec(memory_space=pltpu.VMEM)
ANY = pl.BlockSpec(memory_space=pl.ANY)


def pack_kernel(chunk, table, lengths, source, target, pool, fresh, left, right, page_sem):
    ctx_pages = table.shape[1]
    page_len = pool.shape[1]
    tokens = ctx_pages * page_len
    outs = (left, right)

    def one_page(p, carry):
        for side in range(2):
            for k, step in enumerate(chunk):
                slot = jnp.maximum(source[0, step, side], 0)
                pltpu.make_async_copy(
                    pool.at[table[slot, p]],
                    outs[side].at[pl.ds(k * tokens + p * page_len, page_len)],
                    page_sem.at[side],
                ).start()
        return carry

    lax.fori_loop(0, ctx_pages, one_page, 0)
    for side in range(2):
        filled = outs[side].at[pl.ds(0, len(chunk) * tokens)]
        pltpu.make_async_copy(filled, filled, page_sem.at[side]).wait()
        for k, step in enumerate(chunk):
            slot = jnp.maximum(source[0, step, side], 0)
            for early in range(step):
                outs[side][k * tokens + lengths[slot] + early] = fresh[early, slot]
        if 0 in chunk:
            lane = lax.broadcasted_iota(jnp.int32, pool.shape[2:], 1)
            meta = jnp.zeros(pool.shape[2:], jnp.int32)
            for s in range(source.shape[1]):
                moved = source[0, s, side]
                place = jnp.where(moved >= 0, target[0, s, side] + 1, 0)
                meta = jnp.where(lane == 2 * s, place, meta)
                meta = jnp.where(lane == 2 * s + 1, lengths[jnp.maximum(moved, 0)], meta)
            outs[side][len(chunk) * tokens] = meta.astype(jnp.float32).astype(pool.dtype)


def pack(chunk, table, lengths, source, target, pool, fresh):
    tokens = len(chunk) * table.shape[1] * pool.shape[1]
    row = jax.ShapeDtypeStruct((tokens + (0 in chunk),) + pool.shape[2:], pool.dtype)
    nbytes = 4 * tokens * pool.shape[2] * pool.shape[3] * 2
    return pl.pallas_call(
        functools.partial(pack_kernel, chunk),
        out_shape=(row, row),
        in_specs=[SMEM, SMEM, SMEM, SMEM, ANY, ANY if chunk == (0,) else VMEM],
        out_specs=(VMEM, VMEM),
        scratch_shapes=[pltpu.SemaphoreType.DMA((2,))],
        compiler_params=pltpu.CompilerParams(vmem_limit_bytes=32 * 1024 * 1024),
        cost_estimate=pl.CostEstimate(flops=0, bytes_accessed=nbytes, transcendentals=0),
    )(table, lengths, source, target, pool, fresh)


def attend(rows, query, out, slot, base, first, low, high):
    kv_heads, columns, _ = rows.shape
    total_rows = query.shape[2]
    steps = out.shape[1]
    group = total_rows // steps
    skip = first * group
    shape = (total_rows - skip, columns)
    row_step = lax.broadcasted_iota(jnp.int32, shape, 0) // group + first
    column = lax.broadcasted_iota(jnp.int32, shape, 1)
    seen = (column % 2 == 0) & (column // 2 <= base + row_step)
    step_of = lax.broadcasted_iota(jnp.int32, (shape[0], HD), 0) // group + first
    live = (step_of >= low) & (step_of < high)
    results = []
    scores = [
        lax.dot_general(
            query[slot, head, skip:], rows[head], (((1,), (1,)), ((), ())), preferred_element_type=jnp.float32
        )
        for head in range(kv_heads)
    ]
    for head in range(kv_heads):
        score = jnp.where(seen, scores[head] * HD ** (-0.5), -jnp.inf)
        terms = jnp.exp(score - jnp.max(score, axis=1, keepdims=True))
        total = jnp.sum(terms, axis=1, keepdims=True)
        weights = pltpu.roll(terms, 1, 1).astype(jnp.bfloat16)
        result = jnp.dot(weights, rows[head], preferred_element_type=jnp.float32) / total
        results.append(jnp.where(live, result, 0.0))
    for head in range(kv_heads):
        for s in range(first, steps):
            for g in range(group):
                r = (s - first) * group + g
                lane = (head * group + g) * HD
                out[slot, s : s + 1, lane : lane + HD] = results[head][r : r + 1]


def local_kernel(table, lengths, source, pool, fresh, query, cache, attended, rows, held, out, out_sem, held_sem, row_sem):
    slots, ctx_pages = table.shape
    page_len = pool.shape[1]
    kv_heads = rows.shape[1]
    steps = fresh.shape[0]

    def load_slot(c, carry):
        def load_page(p, carry):
            pltpu.make_async_copy(
                pool.at[table[c, p]], held.at[c, pl.ds(p * page_len, page_len)], held_sem.at[c]
            ).start()
            return carry

        return lax.fori_loop(0, ctx_pages, load_page, carry)

    lax.fori_loop(0, slots, load_slot, 0)

    def leave_step(c):
        leave = jnp.int32(steps)
        for s in range(steps):
            for side in range(2):
                leave = jnp.where(source[0, s, side] == c, s, leave)
        return jnp.where(lengths[c] > 0, leave, 0)

    def split(c):
        pltpu.make_async_copy(held.at[c], held.at[c], held_sem.at[c]).wait()
        high = leave_step(c)
        for s in range(steps):

            @pl.when(s < high)
            def _():
                held[c, lengths[c] + s] = fresh[s, c]

        for head in range(kv_heads):
            pltpu.make_async_copy(
                held.at[c, :, :, pl.ds(head * HD, HD)], rows.at[c % 2, head], row_sem.at[c % 2]
            ).start()

        def store_page(p, carry):
            pltpu.make_async_copy(
                held.at[c, pl.ds(p * page_len, page_len)], cache.at[table[c, p]], out_sem
            ).start()
            return carry

        lax.fori_loop(0, ctx_pages, store_page, 0)

    split(0)

    def work(c, carry):
        @pl.when(c + 1 < slots)
        def _():
            split(c + 1)

        buffer = rows.at[c % 2]
        pltpu.make_async_copy(buffer, buffer, row_sem.at[c % 2]).wait()
        attend(
            buffer.reshape(kv_heads, ctx_pages * page_len * 2, HD), query, out, c, lengths[c], 0, 0, leave_step(c)
        )
        attended[c] = out[c].astype(attended.dtype)
        return carry

    lax.fori_loop(0, slots, work, 0)
    pltpu.make_async_copy(cache, cache, out_sem).wait()


def local(table, lengths, source, pool, fresh, query):
    slots, ctx_pages = table.shape
    tokens = ctx_pages * pool.shape[1]
    kv_heads = query.shape[1]
    steps = fresh.shape[0]
    width = kv_heads * query.shape[2] // steps * HD
    return pl.pallas_call(
        local_kernel,
        out_shape=(
            jax.ShapeDtypeStruct(pool.shape, pool.dtype),
            jax.ShapeDtypeStruct((slots, steps, width), jnp.bfloat16),
        ),
        in_specs=[SMEM, SMEM, SMEM, ANY, VMEM, VMEM],
        out_specs=(ANY, VMEM),
        scratch_shapes=[
            pltpu.VMEM((2, kv_heads, tokens, 2, HD), pool.dtype),
            pltpu.VMEM((slots, tokens) + pool.shape[2:], pool.dtype),
            pltpu.VMEM((slots, steps, width), jnp.float32),
            pltpu.SemaphoreType.DMA,
            pltpu.SemaphoreType.DMA((slots,)),
            pltpu.SemaphoreType.DMA((2,)),
        ],
        compiler_params=pltpu.CompilerParams(vmem_limit_bytes=32 * 1024 * 1024),
        cost_estimate=pl.CostEstimate(flops=10**9, bytes_accessed=60 * 10**6, transcendentals=10**5),
    )(table, lengths, source, pool, fresh, query)


def arrive_kernel(chunk, table, meta_left, meta_right, left, right, fresh, query, cache_in, before, cache, attended, rows, held, out, out_sem, held_sem, row_sem):
    ctx_pages = table.shape[1]
    page_len = cache.shape[1]
    kv_heads = rows.shape[1]
    steps = fresh.shape[0]
    tokens = held.shape[1]
    items = []
    for k, step in enumerate(chunk):
        for received, meta in ((left, meta_left), (right, meta_right)):
            items.append(
                (len(items), step, received.at[pl.ds(k * tokens, tokens)], meta[step, 0] - 1, meta[step, 1])
            )

    for i, step, row, slot, base in items:

        @pl.when(slot >= 0)
        def _():
            pltpu.make_async_copy(row, held.at[i], held_sem.at[i]).start()
            for head in range(kv_heads):
                pltpu.make_async_copy(
                    row.at[:, :, pl.ds(head * HD, HD)], rows.at[i, head], row_sem.at[i]
                ).start()

    attended[...] = before[...]
    for i, step, row, slot, base in items:

        @pl.when(slot >= 0)
        def _():
            pltpu.make_async_copy(row, held.at[i], held_sem.at[i]).wait()
            for s in range(step, steps):
                held[i, base + s] = fresh[s, slot]

            def store_page(p, carry):
                pltpu.make_async_copy(
                    held.at[i, pl.ds(p * page_len, page_len)], cache.at[table[slot, p]], out_sem.at[i]
                ).start()
                return carry

            lax.fori_loop(0, ctx_pages, store_page, 0)
            pltpu.make_async_copy(rows.at[i], rows.at[i], row_sem.at[i]).wait()
            for s in range(step, steps):
                for head in range(kv_heads):
                    rows[i, head, base + s] = fresh[s, slot, :, head * HD : (head + 1) * HD]
            out[i] = jnp.zeros_like(out[i])
            attend(
                rows.at[i].reshape(kv_heads, tokens * 2, HD),
                query.at[pl.ds(slot, 1)], out.at[pl.ds(i, 1)], 0, base, step, step, steps,
            )
            attended[slot] = out[i].astype(attended.dtype)

    for i, step, row, slot, base in items:

        @pl.when(slot >= 0)
        def _():
            pltpu.make_async_copy(held.at[i], held.at[i], out_sem.at[i]).wait()


def arrive(chunk, table, meta_left, meta_right, left, right, fresh, query, cache, attended):
    kv_heads = query.shape[1]
    tokens = table.shape[1] * cache.shape[1]
    count = 2 * len(chunk)
    return pl.pallas_call(
        functools.partial(arrive_kernel, chunk),
        out_shape=(
            jax.ShapeDtypeStruct(cache.shape, cache.dtype),
            jax.ShapeDtypeStruct(attended.shape, attended.dtype),
        ),
        in_specs=[SMEM, SMEM, SMEM, ANY, ANY, VMEM, VMEM, ANY, VMEM],
        out_specs=(ANY, VMEM),
        input_output_aliases={7: 0},
        scratch_shapes=[
            pltpu.VMEM((count, kv_heads, tokens, 2, HD), cache.dtype),
            pltpu.VMEM((count, tokens) + cache.shape[2:], cache.dtype),
            pltpu.VMEM((count,) + attended.shape[1:], jnp.float32),
            pltpu.SemaphoreType.DMA((count,)),
            pltpu.SemaphoreType.DMA((count,)),
            pltpu.SemaphoreType.DMA((count,)),
        ],
        compiler_params=pltpu.CompilerParams(vmem_limit_bytes=32 * 1024 * 1024),
        cost_estimate=pl.CostEstimate(flops=10**8, bytes_accessed=10 * 10**6, transcendentals=10**5),
    )(table, meta_left, meta_right, left, right, fresh, query, cache, attended)


def body(kv_pool, page_table, lengths, move_source, move_slot, queries, new_kv):
    slots = page_table.shape[0]
    steps = queries.shape[0]
    kv_heads = kv_pool.shape[3] // HD
    group = queries.shape[2] // HD // kv_heads
    count = lax.axis_size("inst")

    def shift(value, by):
        return lax.ppermute(value, "inst", [(i, (i + by) % count) for i in range(count)])

    chunks = [(0,), tuple(range(1, steps - 1)), (steps - 1,)]
    arrived = []
    for chunk in chunks:
        up, down = pack(chunk, page_table, lengths, move_source, move_slot, kv_pool, new_kv)
        if chunk == chunks[0]:
            up, down, queries = lax.optimization_barrier((up, down, queries))
        if chunk == chunks[1]:
            query = queries.reshape(steps, slots, kv_heads, group, HD).transpose(1, 2, 0, 3, 4)
            query = query.reshape(slots, kv_heads, steps * group, HD)
            cache, attended = local(page_table, lengths, move_source, kv_pool, new_kv, query)
            lengths, attended = lax.optimization_barrier((lengths, attended))
        arrived.append((shift(up, 1), shift(down, -1)))
    meta_left, meta_right = (
        row[-1, 0, : 2 * steps].astype(jnp.int32).reshape(steps, 2) for row in arrived[0]
    )
    for chunk, received in zip(chunks, arrived):
        cache, attended = arrive(
            chunk, page_table, meta_left, meta_right, *received, new_kv, query, cache, attended
        )
    return attended.transpose(1, 0, 2), cache


def solution(mesh):
    in_specs = (
        P(("group", "inst"), None, None, "tp"),
        P(("group", "inst"), None),
        P(("group", "inst")),
        P(("group", "inst"), None, None),
        P(("group", "inst"), None, None),
        P(None, ("group", "inst"), "tp"),
        P(None, ("group", "inst"), None, "tp"),
    )
    out_specs = (P(None, ("group", "inst"), "tp"), P(("group", "inst"), None, None, "tp"))
    return jax.shard_map(body, mesh=mesh, in_specs=in_specs, out_specs=out_specs, check_vma=False)
```

time: 251 us -> 111 us (0.44)
  Pallas kernels: 214 us -> 47.4 us
  waiting for transfers between devices: 1.33 us -> 37.7 us
  starting transfers between devices: 25.4 us -> 16.4 us
    pallas_call x8 -> x6, Pallas kernels: 190 us -> 25.8 us  [the longest x3 13.3 us: arrive(): pl.pallas_call(functools.partial(arrive_kernel, chunk), out_shape=(jax.Sh...]
    ppermute x10 -> x6, waiting for transfers between devices: 1.33 us -> 37.7 us  [shift(): lax.ppermute(value, 'inst', [(i, (i + by) % count) for i in range(count)])]
    ppermute x10 -> x6, starting transfers between devices: 25.4 us -> 16.4 us  [shift(): lax.ppermute(value, 'inst', [(i, (i + by) % count) for i in range(count)])]
    unnamed x18 -> x22, local copies, waits for them, and re-layouts: 4.83 us -> 8.75 us
    pallas_call x1, Pallas kernels: 24.4 us -> 21.6 us  [local(): pl.pallas_call(local_kernel, out_shape=(jax.ShapeDtypeStruct(pool.shape,...]
    reshape x2, local copies, waits for them, and re-layouts: 3.07 us -> 0.4 us  [body(): queries.reshape(steps, slots, kv_heads, group, HD).transpose(1, 2, 0, 3, 4)]
  transfers between devices with their start and end apart: 10 -> 6, of which waited for: 1 -> 2; matrix products, arithmetic and copies ran while one was open for 2% -> 1% of each run, Pallas kernels for 64% -> 33%
where the time goes in v1:
time: 111 us; the launch traced here: 112 us
  Pallas kernels  47.4 us (43%)
  waiting for transfers between devices  37.7 us (34%)
  starting transfers between devices  16.4 us (15%)
  local copies, waits for them, and re-layouts  9.33 us (8%)
    ppermute x6, waiting for transfers between devices, shift(): lax.ppermute(value, 'inst', [(i, (i + by) % count) for i in range(count)])  37.7 us
    pallas_call x1, Pallas kernels, local(): pl.pallas_call(local_kernel, out_shape=(jax.ShapeDtypeStruct(pool.shape,...  21.6 us
    ppermute x6, starting transfers between devices, shift(): lax.ppermute(value, 'inst', [(i, (i + by) % count) for i in range(count)])  16.4 us
    pallas_call x3, Pallas kernels, arrive(): pl.pallas_call(functools.partial(arrive_kernel, chunk), out_shape=(jax.Sh...  13.3 us
    pallas_call x3, Pallas kernels, pack(): pl.pallas_call(functools.partial(pack_kernel, chunk), out_shape=(row, row...  12.5 us
    unnamed x22, local copies, waits for them, and re-layouts  8.75 us
  transfers between devices with their start and end apart: 6, of which 2 were waited for; matrix products, arithmetic and copies ran while one was open for 1% of the time, Pallas kernels for 33%

profile of v1, /device:TPU:0, one launch (start us, length us, event | category | flops | bytes accessed | tf_op | source)
XLA Modules:
  0.0 112.3 jit_solution(14744067059637112315)
XLA Ops:
  0.6 0.8 copy.20.source
  1.4 0.8 copy.21.target
  2.2 0.0 copy-start
  2.2 2.5 %copy-done = bf16[160,16,2,512]{3,2,1,0:T(2,128)(2,1)S(1)} copy-done((bf16[160,16,2,512]{3,2,1,0:T(2,128)(2,1)S(1)}, bf16[160,16,2,512]{3,2,1,0:T(2,128)(2,1)}, u32[]{:S(2)}) %copy-start) | copy-done | bytes 5242904
  4.6 0.0 copy-start.3
  4.6 0.9 copy-done.3
  5.5 0.0 copy-start.5
  5.5 0.7 copy-done.5
  6.2 0.0 copy-start.7
  6.2 0.7 copy-done.7
  6.9 0.0 copy-start.9
  6.9 0.0 copy-start.4
  6.9 0.0 copy-start.6
  6.9 0.0 copy-start.8
  6.9 5.5 %shard_map.89 = (bf16[512,2,512]{2,1,0:T(2,128)(2,1)}, bf16[512,2,512]{2,1,0:T(2,128)(2,1)}) custom-call(s32[10,16]{1,0:T(8,128)S(1)} %copy-done.5, s32[10]{0:T(128)S(1)} %copy-done.7, s32[1,4,2]{2,1,0:T(4,128)S(1)} %copy.20.source, s32[1,4,2]{2,1,0:T(4,128)S(1)} %copy.21.target, bf16[160,16,2,512]{3,2,1,0:T(2,128)(2,1)S(1)} %copy-done, ...), custom_call_target="tpu_custom_call" | custom-call | bytes 4194304 | tf_op jit(solution)/shard_map/pallas_call | solution.py:56
  12.4 3.0 %collective-permute-start.4 = (bf16[512,2,512]{2,1,0:T(2,128)(2,1)}, bf16[512,2,512]{2,1,0:T(2,128)(2,1)S(1)}, u32[]{:S(2)}, u32[]{:S(2)}) collective-permute-start(bf16[512,2,512]{2,1,0:T(2,128)(2,1)} %get-tuple-element.30), channel_id=1, source_target_pairs={{0,2},{2,4},{4,6},{6,8},{8,10},{10,12},{12,14},{14,0},{1,3},{3,5},... | collective-permute-start | bytes 3145736 | tf_op jit(solution)/shard_map/ppermute | solution.py:284
  15.4 3.1 %collective-permute-start.5 = (bf16[512,2,512]{2,1,0:T(2,128)(2,1)}, bf16[512,2,512]{2,1,0:T(2,128)(2,1)S(1)}, u32[]{:S(2)}, u32[]{:S(2)}) collective-permute-start(bf16[512,2,512]{2,1,0:T(2,128)(2,1)} %get-tuple-element.31), channel_id=1, source_target_pairs={{0,14},{2,0},{4,2},{6,4},{8,6},{10,8},{12,10},{14,12},{1,15},{3,1}... | collective-permute-start | bytes 3145736 | tf_op jit(solution)/shard_map/ppermute | solution.py:284
  18.5 3.5 %shard_map.86 = (bf16[257,2,512]{2,1,0:T(2,128)(2,1)}, bf16[257,2,512]{2,1,0:T(2,128)(2,1)}) custom-call(s32[10,16]{1,0:T(8,128)S(1)} %copy-done.5, s32[10]{0:T(128)S(1)} %copy-done.7, s32[1,4,2]{2,1,0:T(4,128)S(1)} %copy.20.source, s32[1,4,2]{2,1,0:T(4,128)S(1)} %copy.21.target, bf16[160,16,2,512]{3,2,1,0:T(2,128)(2,1)S(1)} %copy-done, ...), custom_call_target="tpu_custom_call" | custom-call | bytes 2097152 | tf_op jit(solution)/shard_map/pallas_call | solution.py:56
  22.1 0.1 collective-permute-start
  22.1 4.7 %collective-permute-start.1 = (bf16[257,2,512]{2,1,0:T(2,128)(2,1)}, bf16[257,2,512]{2,1,0:T(2,128)(2,1)}, u32[]{:S(2)}, u32[]{:S(2)}) collective-permute-start(bf16[257,2,512]{2,1,0:T(2,128)(2,1)} %get-tuple-element.24), channel_id=1, source_target_pairs={{0,14},{2,0},{4,2},{6,4},{8,6},{10,8},{12,10},{14,12},{1,15},{3,1}... | collective-permute-start | bytes 1579016 | tf_op jit(solution)/shard_map/ppermute | solution.py:284
  26.8 0.0 copy-done.9
  26.8 0.3 reshape.18
  27.2 0.1 copy.29
  27.3 0.0 copy-done.4
  27.3 0.0 copy-done.6
  27.3 0.0 copy-done.8
  27.3 0.0 copy-start.1
  27.3 2.5 %copy-done.1 = bf16[160,16,2,512]{3,2,1,0:T(2,128)(2,1)S(1)} copy-done((bf16[160,16,2,512]{3,2,1,0:T(2,128)(2,1)S(1)}, bf16[160,16,2,512]{3,2,1,0:T(2,128)(2,1)}, u32[]{:S(2)}) %copy-start.1) | copy-done | bytes 5242904
  29.8 0.0 copy-start.2
  29.8 21.6 %shard_map.87 = (bf16[160,16,2,512]{3,2,1,0:T(2,128)(2,1)}, bf16[10,4,4096]{2,1,0:T(4,128)(2,1)S(1)}) custom-call(s32[10,16]{1,0:T(8,128)S(1)} %copy-done.6, s32[10]{0:T(128)S(1)} %copy-done.8, s32[1,4,2]{2,1,0:T(4,128)S(1)} %copy.20.source, bf16[160,16,2,512]{3,2,1,0:T(2,128)(2,1)S(1)} %copy-done.1, bf16[4,10,2,512]{3,2,1,0:T(2,128)(2,1)S(1)} %copy-done.4, ...), custom_call_target="tpu_custom_call" | custom-call | flops 1000000000 | bytes 60000000 | tf_op jit(solution)/shard_map/pallas_call | solution.py:172
  51.3 0.0 copy-done.2
  51.3 3.5 %shard_map.88 = (bf16[256,2,512]{2,1,0:T(2,128)(2,1)}, bf16[256,2,512]{2,1,0:T(2,128)(2,1)}) custom-call(s32[10,16]{1,0:T(8,128)S(1)} %copy-done.6, s32[10]{0:T(128)S(1)} %copy-done.8, s32[1,4,2]{2,1,0:T(4,128)S(1)} %copy.20.source, s32[1,4,2]{2,1,0:T(4,128)S(1)} %copy.21.target, bf16[160,16,2,512]{3,2,1,0:T(2,128)(2,1)S(1)} %copy-done.2, ...), custom_call_target="tpu_custom_call" | custom-call | bytes 2097152 | tf_op jit(solution)/shard_map/pallas_call | solution.py:56
  54.8 0.1 collective-permute-start.2
  54.9 29.5 %collective-permute-done.left = bf16[257,2,512]{2,1,0:T(2,128)(2,1)S(1)} collective-permute-done((bf16[257,2,512]{2,1,0:T(2,128)(2,1)}, bf16[257,2,512]{2,1,0:T(2,128)(2,1)S(1)}, u32[]{:S(2)}, u32[]{:S(2)}) %collective-permute-start) | collective-permute-done | bytes 526368 | tf_op jit(solution)/shard_map/ppermute | solution.py:284
  84.3 5.4 %collective-permute-start.3 = (bf16[256,2,512]{2,1,0:T(2,128)(2,1)}, bf16[256,2,512]{2,1,0:T(2,128)(2,1)}, u32[]{:S(2)}, u32[]{:S(2)}) collective-permute-start(bf16[256,2,512]{2,1,0:T(2,128)(2,1)} %get-tuple-element.29), channel_id=1, source_target_pairs={{0,14},{2,0},{4,2},{6,4},{8,6},{10,8},{12,10},{14,12},{1,15},{3,1}... | collective-permute-start | bytes 1572872 | tf_op jit(solution)/shard_map/ppermute | solution.py:284
  89.8 0.1 reshape.20.meta_left
  89.9 8.2 %collective-permute-done.1.right = bf16[257,2,512]{2,1,0:T(2,128)(2,1)} collective-permute-done((bf16[257,2,512]{2,1,0:T(2,128)(2,1)}, bf16[257,2,512]{2,1,0:T(2,128)(2,1)}, u32[]{:S(2)}, u32[]{:S(2)}) %collective-permute-start.1) | collective-permute-done | bytes 526368 | tf_op jit(solution)/shard_map/ppermute | solution.py:284
  98.1 0.7 fusion
  98.8 0.1 reshape.21.meta_right
  98.9 3.4 %shard_map.90 = (bf16[160,16,2,512]{3,2,1,0:T(2,128)(2,1)}, bf16[10,4,4096]{2,1,0:T(4,128)(2,1)S(1)}) custom-call(s32[10,16]{1,0:T(8,128)S(1)} %copy-done.6, s32[4,2]{1,0:T(4,128)S(1)} %reshape.20.meta_left, s32[4,2]{1,0:T(4,128)S(1)} %reshape.21.meta_right, bf16[257,2,512]{2,1,0:T(2,128)(2,1)S(1)} %collective-permute-done.left, ...), custom_call_target="tpu_custom_call", output_to_operand_aliasing={{0}: (7, {})} | custom-call | flops 100000000 | bytes 10000000 | tf_op jit(solution)/shard_map/pallas_call | solution.py:254
  102.3 0.0 collective-permute-done.4.left
  102.3 0.0 collective-permute-done.5.right
  102.3 5.7 %shard_map.91 = (bf16[160,16,2,512]{3,2,1,0:T(2,128)(2,1)}, bf16[10,4,4096]{2,1,0:T(4,128)(2,1)S(1)}) custom-call(s32[10,16]{1,0:T(8,128)S(1)} %copy-done.6, s32[4,2]{1,0:T(4,128)S(1)} %reshape.20.meta_left, s32[4,2]{1,0:T(4,128)S(1)} %reshape.21.meta_right, bf16[512,2,512]{2,1,0:T(2,128)(2,1)S(1)} %collective-permute-done.4.left, ...), custom_call_target="tpu_custom_call", output_to_operand_aliasing={{0}: (7, {})} | custom-call | flops 100000000 | bytes 10000000 | tf_op jit(solution)/shard_map/pallas_call | solution.py:254
  108.0 0.0 collective-permute-done.2.left
  108.0 0.0 collective-permute-done.3.right
  108.0 4.3 %shard_map.92 = (bf16[160,16,2,512]{3,2,1,0:T(2,128)(2,1)}, bf16[10,4,4096]{2,1,0:T(4,128)(2,1)}) custom-call(s32[10,16]{1,0:T(8,128)S(1)} %copy-done.6, s32[4,2]{1,0:T(4,128)S(1)} %reshape.20.meta_left, s32[4,2]{1,0:T(4,128)S(1)} %reshape.21.meta_right, bf16[256,2,512]{2,1,0:T(2,128)(2,1)} %collective-permute-done.2.left, ...), custom_call_target="tpu_custom_call", output_to_operand_aliasing={{0}: (7, {})} | custom-call | flops 100000000 | bytes 10000000 | tf_op jit(solution)/shard_map/pallas_call | solution.py:254
  (1 shorter events, 0.0 us)
Async XLA Ops:
  2.2 2.5 %copy-start = (bf16[160,16,2,512]{3,2,1,0:T(2,128)(2,1)S(1)}, bf16[160,16,2,512]{3,2,1,0:T(2,128)(2,1)}, u32[]{:S(2)}) copy-start(bf16[160,16,2,512]{3,2,1,0:T(2,128)(2,1)} %pool.7) | copy-start | bytes 15728644
  4.6 0.9 copy-start.3
  5.5 0.7 copy-start.5
  6.2 0.7 copy-start.7
  6.9 19.9 %copy-start.9 = (bf16[4,10,4096]{2,0,1:T(4,128)(2,1)S(1)}, bf16[4,10,4096]{2,0,1:T(4,128)(2,1)}, u32[]{:S(2)}) copy-start(bf16[4,10,4096]{2,0,1:T(4,128)(2,1)} %param.12) | copy-start | bytes 983044
  6.9 20.4 %copy-start.4 = (bf16[4,10,2,512]{3,2,1,0:T(2,128)(2,1)S(1)}, bf16[4,10,2,512]{3,2,1,0:T(2,128)(2,1)}, u32[]{:S(2)}) copy-start(bf16[4,10,2,512]{3,2,1,0:T(2,128)(2,1)} %fresh.13) | copy-start | bytes 245764
  6.9 20.4 %copy-start.6 = (s32[10,16]{1,0:T(8,128)S(1)}, s32[10,16]{1,0:T(8,128)}, u32[]{:S(2)}) copy-start(s32[10,16]{1,0:T(8,128)} %table.13) | copy-start | bytes 1924
  6.9 20.4 %copy-start.8 = (s32[10]{0:T(128)S(1)}, s32[10]{0:T(128)}, u32[]{:S(2)}) copy-start(s32[10]{0:T(128)} %lengths.6) | copy-start | bytes 124
  12.4 89.9 %collective-permute-start.4 = (bf16[512,2,512]{2,1,0:T(2,128)(2,1)}, bf16[512,2,512]{2,1,0:T(2,128)(2,1)S(1)}, u32[]{:S(2)}, u32[]{:S(2)}) collective-permute-start(bf16[512,2,512]{2,1,0:T(2,128)(2,1)} %get-tuple-element.30), channel_id=1, source_target_pairs={{0,2},{2,4},{4,6},{6,8},{8,10},{10,12},{12,14},{14,0},{1,3},{3,5},... | collective-permute-start | bytes 3145736 | tf_op jit(solution)/shard_map/ppermute | solution.py:284
  15.4 86.8 %collective-permute-start.5 = (bf16[512,2,512]{2,1,0:T(2,128)(2,1)}, bf16[512,2,512]{2,1,0:T(2,128)(2,1)S(1)}, u32[]{:S(2)}, u32[]{:S(2)}) collective-permute-start(bf16[512,2,512]{2,1,0:T(2,128)(2,1)} %get-tuple-element.31), channel_id=1, source_target_pairs={{0,14},{2,0},{4,2},{6,4},{8,6},{10,8},{12,10},{14,12},{1,15},{3,1}... | collective-permute-start | bytes 3145736 | tf_op jit(solution)/shard_map/ppermute | solution.py:284
  22.1 62.3 %collective-permute-start = (bf16[257,2,512]{2,1,0:T(2,128)(2,1)}, bf16[257,2,512]{2,1,0:T(2,128)(2,1)S(1)}, u32[]{:S(2)}, u32[]{:S(2)}) collective-permute-start(bf16[257,2,512]{2,1,0:T(2,128)(2,1)} %get-tuple-element.23), channel_id=1, source_target_pairs={{0,2},{2,4},{4,6},{6,8},{8,10},{10,12},{12,14},{14,0},{1,3},{3,5},... | collective-permute-start | bytes 1579016 | tf_op jit(solution)/shard_map/ppermute | solution.py:284
  22.1 76.0 %collective-permute-start.1 = (bf16[257,2,512]{2,1,0:T(2,128)(2,1)}, bf16[257,2,512]{2,1,0:T(2,128)(2,1)}, u32[]{:S(2)}, u32[]{:S(2)}) collective-permute-start(bf16[257,2,512]{2,1,0:T(2,128)(2,1)} %get-tuple-element.24), channel_id=1, source_target_pairs={{0,14},{2,0},{4,2},{6,4},{8,6},{10,8},{12,10},{14,12},{1,15},{3,1}... | collective-permute-start | bytes 1579016 | tf_op jit(solution)/shard_map/ppermute | solution.py:284
  27.3 2.5 %copy-start.1 = (bf16[160,16,2,512]{3,2,1,0:T(2,128)(2,1)S(1)}, bf16[160,16,2,512]{3,2,1,0:T(2,128)(2,1)}, u32[]{:S(2)}) copy-start(bf16[160,16,2,512]{3,2,1,0:T(2,128)(2,1)} %pool.7) | copy-start | bytes 15728644
  29.8 21.6 %copy-start.2 = (bf16[160,16,2,512]{3,2,1,0:T(2,128)(2,1)S(1)}, bf16[160,16,2,512]{3,2,1,0:T(2,128)(2,1)}, u32[]{:S(2)}) copy-start(bf16[160,16,2,512]{3,2,1,0:T(2,128)(2,1)} %pool.7) | copy-start | bytes 15728644
  54.8 53.2 %collective-permute-start.2 = (bf16[256,2,512]{2,1,0:T(2,128)(2,1)}, bf16[256,2,512]{2,1,0:T(2,128)(2,1)}, u32[]{:S(2)}, u32[]{:S(2)}) collective-permute-start(bf16[256,2,512]{2,1,0:T(2,128)(2,1)} %get-tuple-element.28), channel_id=1, source_target_pairs={{0,2},{2,4},{4,6},{6,8},{8,10},{10,12},{12,14},{14,0},{1,3},{3,5},... | collective-permute-start | bytes 1572872 | tf_op jit(solution)/shard_map/ppermute | solution.py:284
  84.3 23.6 %collective-permute-start.3 = (bf16[256,2,512]{2,1,0:T(2,128)(2,1)}, bf16[256,2,512]{2,1,0:T(2,128)(2,1)}, u32[]{:S(2)}, u32[]{:S(2)}) collective-permute-start(bf16[256,2,512]{2,1,0:T(2,128)(2,1)} %get-tuple-element.29), channel_id=1, source_target_pairs={{0,14},{2,0},{4,2},{6,4},{8,6},{10,8},{12,10},{14,12},{1,15},{3,1}... | collective-permute-start | bytes 1572872 | tf_op jit(solution)/shard_map/ppermute | solution.py:284
